TPU v7x, 32 devices: a whole 2x2x4 slice. The times are simulated.
32 devices in a mesh: leaf: 8 (over y, x, core), rank: 4 (over z).
Axes of the slice: x: 2, y: 2, z: 4, core: 2. Of those that a mesh axis runs over, the one named last changes fastest.
Arguments:
- load_vectors: bfloat16 [32, 4, 256], P('leaf'), may hold values from -6 to 6
- cluster_order: int32 [32, 256], P('leaf'), may hold values from 0 to 255, each once within a row
- block_present: int32 [8, 32], P(None, 'leaf'), may hold values 0 or 1
- factors: bfloat16 [8, 32, 2, 256, 256], P(None, 'leaf', None, 'rank'), may hold values from -0.25 to 0.25
Outputs:
- applied: float32 [32, 4, 256], P('leaf')
Inputs may be any that keep to these rules, and one draw needn't show every extreme that they name: `cluster_order`: each row is a permutation of 0 .. 255.
All inputs are finite; a program needn't handle non-finite values. No bound on the sum of `block_present` on one device may be relied on, other than what follows from the above.
Results may differ from a plain program's by a relative error of at most 0.012.
Values may be sent and summed in bfloat16 or wider, within the bound.
A program may use at most 64 MiB of HBM per device.

v0:
```python
import jax
import jax.numpy as jnp
from jax import lax
from jax.sharding import PartitionSpec as P

LEVELS = 8


def swapped(block, axis, distance):
    count = lax.axis_size(axis)
    route = []
    for low in range(count):
        high = low | 1 << distance
        if high != low and high < count:
            route += [(low, high), (high, low)]
    return lax.ppermute(block, axis, route)


def partner_of(own_cols, level_bit, local_bits):
    if level_bit < local_bits:
        shaped = own_cols.reshape(
            (own_cols.shape[0] >> level_bit + 1, 2, 1 << level_bit) + own_cols.shape[1:]
        )
        return jnp.flip(shaped, 1).reshape(own_cols.shape)
    return swapped(own_cols, "leaf", level_bit - local_bits)


def level_terms(own_cols, weights, present, level_bit, local_bits):
    partner = partner_of(own_cols, level_bit, local_bits)
    own_term = jnp.einsum(
        "blc,bco->blo", own_cols, weights[:, 0], preferred_element_type=jnp.float32
    )
    off_term = jnp.einsum(
        "blc,bco->blo", partner, weights[:, 1], preferred_element_type=jnp.float32
    )
    return own_term + present.astype(jnp.float32)[:, None, None] * off_term


def local(load_vectors, cluster_order, block_present, factors):
    blocks = load_vectors.shape[0]
    local_bits = blocks.bit_length() - 1
    tree_bits = local_bits + lax.axis_size("leaf").bit_length() - 1
    columns = factors.shape[3]
    first_col = lax.axis_index("rank") * columns
    current = jnp.take_along_axis(load_vectors, cluster_order[:, None, :], axis=2).astype(
        jnp.float32
    )
    for level_idx in range(LEVELS):
        level_bit = (tree_bits - 1 - level_idx) % tree_bits
        rounded = current.astype(jnp.bfloat16)
        own_cols = lax.dynamic_slice_in_dim(rounded, first_col, columns, 2)
        terms = level_terms(
            own_cols, factors[level_idx], block_present[level_idx], level_bit, local_bits
        )
        current = lax.psum(terms, "rank")
    inverse = jnp.argsort(cluster_order, axis=1)
    return jnp.take_along_axis(current, inverse[:, None, :], axis=2)


def solution(mesh):
    in_specs = (
        P("leaf", None, None),
        P("leaf", None),
        P(None, "leaf"),
        P(None, "leaf", None, "rank", None),
    )
    out_specs = P("leaf", None, None)
    return jax.shard_map(local, mesh=mesh, in_specs=in_specs, out_specs=out_specs, check_vma=False)
```

profile of v0, /device:TPU:0, one launch (start us, length us, event | category | flops | bytes accessed | tf_op | source)
XLA Modules:
  0.0 185.0 jit_solution(10752610109844792322)
XLA Ops:
  6.5 0.6 iota.7
  7.3 1.6 fusion.20
  8.9 0.3 convert_reduce_fusion
  9.3 0.2 copy.16
  9.7 2.9 %sort.19.cloned.1.call-done = (s32[4,256]{1,0:T(4,128)}, s32[4,256]{1,0:T(4,128)}) async-done(((s32[4,256]{1,0:T(4,128)}, s32[4,256]{1,0:T(4,128)}), (s32[4,256]{1,0:T(4,128)}, s32[4,256]{1,0:T(4,128)})) %sort.19.cloned.1.call-update) | async-done | bytes 8208 | tf_op jit(solution)/shard_map/jit(argsort)/sort | solution.py:56
  12.6 0.7 compare_and_fusion
  13.2 0.7 fusion.16
  13.9 5.8 %gather_fusion = bf16[1024,4]{1,0:T(8,128)(2,1)S(1)} fusion(bf16[4,4,256]{1,2,0:T(8,128)(2,1)S(1)} %copy.16, s32[1024]{0:T(1024)S(1)} %bitcast.113), kind=kCustom, calls=%fused_computation | custom fusion | bytes 24576 | tf_op jit(solution)/shard_map/jit(take_along_axis)/gather | solution.py:45
  19.8 0.1 copy.17
  20.1 3.0 %collective-permute-start = (bf16[4,4,64]{2,1,0:T(4,128)(2,1)S(1)}, bf16[4,4,64]{2,1,0:T(4,128)(2,1)S(1)}, u32[]{:S(2)}, u32[]{:S(2)}) collective-permute-start(bf16[4,4,64]{2,1,0:T(4,128)(2,1)S(1)} %fusion.18), channel_id=1, source_target_pairs={{0,16},{16,0},{4,20},{20,4},{8,24},{24,8},{12,28},{28,12},{1,17},{... | collective-permute-start | bytes 6152 | tf_op jit(solution)/shard_map/ppermute | solution.py:16
  23.0 0.2 fusion.15
  23.2 1.4 collective-permute-done
  24.7 19.6 %psum.56 = bf16[4,4,256]{2,1,0:T(4,128)(2,1)S(1)} all-reduce(f32[4,4,256]{2,1,0:T(4,128)S(1)} %fusion.7), channel_id=1, replica_groups=mesh['leaf'=8,'rank'=4] {'rank'}, use_global_device_ids=true, to_apply=%region_1.2 | all-reduce | flops 4096 | bytes 24576 | tf_op jit(solution)/shard_map/psum | solution.py:55
  44.3 1.5 collective-permute-start.1
  46.0 2.0 %collective-permute-done.1 = bf16[4,4,64]{2,1,0:T(4,128)(2,1)S(1)} collective-permute-done((bf16[4,4,64]{2,1,0:T(4,128)(2,1)S(1)}, bf16[4,4,64]{2,1,0:T(4,128)(2,1)S(1)}, u32[]{:S(2)}, u32[]{:S(2)}) %collective-permute-start.1) | collective-permute-done | bytes 2080 | tf_op jit(solution)/shard_map/ppermute | solution.py:16
  48.0 15.6 %psum.57 = bf16[4,4,256]{2,1,0:T(4,128)(2,1)S(1)} all-reduce(f32[4,4,256]{2,1,0:T(4,128)S(1)} %fusion.6), channel_id=1, replica_groups=mesh['leaf'=8,'rank'=4] {'rank'}, use_global_device_ids=true, to_apply=%region_2.3 | all-reduce | flops 4096 | bytes 24576 | tf_op jit(solution)/shard_map/psum | solution.py:55
  63.8 1.0 collective-permute-done.2
  65.0 16.4 %psum.58 = bf16[4,4,256]{2,1,0:T(4,128)(2,1)S(1)} all-reduce(f32[4,4,256]{2,1,0:T(4,128)S(1)} %fusion.5), channel_id=1, replica_groups=mesh['leaf'=8,'rank'=4] {'rank'}, use_global_device_ids=true, to_apply=%region_3.4 | all-reduce | flops 4096 | bytes 24576 | tf_op jit(solution)/shard_map/psum | solution.py:55
  81.6 15.6 %psum.59 = bf16[4,4,256]{2,1,0:T(4,128)(2,1)S(1)} all-reduce(f32[4,4,256]{2,1,0:T(4,128)S(1)} %fusion.4), channel_id=1, replica_groups=mesh['leaf'=8,'rank'=4] {'rank'}, use_global_device_ids=true, to_apply=%region_4.5 | all-reduce | flops 4096 | bytes 24576 | tf_op jit(solution)/shard_map/psum | solution.py:55
  97.6 16.3 %psum.60 = bf16[4,4,256]{2,1,0:T(4,128)(2,1)S(1)} all-reduce(f32[4,4,256]{2,1,0:T(4,128)S(1)} %fusion.3), channel_id=1, replica_groups=mesh['leaf'=8,'rank'=4] {'rank'}, use_global_device_ids=true, to_apply=%region_5.6 | all-reduce | flops 4096 | bytes 24576 | tf_op jit(solution)/shard_map/psum | solution.py:55
  113.9 1.5 collective-permute-start.3
  115.6 2.0 %collective-permute-done.3 = bf16[4,4,64]{2,1,0:T(4,128)(2,1)S(1)} collective-permute-done((bf16[4,4,64]{2,1,0:T(4,128)(2,1)S(1)}, bf16[4,4,64]{2,1,0:T(4,128)(2,1)S(1)}, u32[]{:S(2)}, u32[]{:S(2)}) %collective-permute-start.3) | collective-permute-done | bytes 2080 | tf_op jit(solution)/shard_map/ppermute | solution.py:16
  117.6 15.6 %psum.61 = bf16[4,4,256]{2,1,0:T(4,128)(2,1)S(1)} all-reduce(f32[4,4,256]{2,1,0:T(4,128)S(1)} %fusion.2), channel_id=1, replica_groups=mesh['leaf'=8,'rank'=4] {'rank'}, use_global_device_ids=true, to_apply=%region_6.7 | all-reduce | flops 4096 | bytes 24576 | tf_op jit(solution)/shard_map/psum | solution.py:55
  133.4 1.5 collective-permute-start.4
  135.0 2.0 %collective-permute-done.4 = bf16[4,4,64]{2,1,0:T(4,128)(2,1)S(1)} collective-permute-done((bf16[4,4,64]{2,1,0:T(4,128)(2,1)S(1)}, bf16[4,4,64]{2,1,0:T(4,128)(2,1)S(1)}, u32[]{:S(2)}, u32[]{:S(2)}) %collective-permute-start.4) | collective-permute-done | bytes 2080 | tf_op jit(solution)/shard_map/ppermute | solution.py:16
  137.1 16.3 %psum.62 = bf16[4,4,256]{2,1,0:T(4,128)(2,1)S(1)} all-reduce(f32[4,4,256]{2,1,0:T(4,128)S(1)} %fusion.1), channel_id=1, replica_groups=mesh['leaf'=8,'rank'=4] {'rank'}, use_global_device_ids=true, to_apply=%region_7.8 | all-reduce | flops 4096 | bytes 24576 | tf_op jit(solution)/shard_map/psum | solution.py:55
  153.6 1.0 collective-permute-done.5
  154.7 15.6 %psum.63 = f32[4,4,256]{2,1,0:T(4,128)S(1)} all-reduce(f32[4,4,256]{2,1,0:T(4,128)S(1)} %fusion), channel_id=1, replica_groups=mesh['leaf'=8,'rank'=4] {'rank'}, use_global_device_ids=true, to_apply=%region_8.9 | all-reduce | flops 4096 | bytes 32768 | tf_op jit(solution)/shard_map/psum | solution.py:55
  170.3 0.2 copy.26
  170.5 6.8 %gather_fusion.1 = f32[1024,4]{1,0:T(8,128)S(1)} fusion(f32[4,4,256]{1,2,0:T(8,128)S(1)} %copy.26, s32[1024]{0:T(1024)S(1)} %bitcast.114), kind=kCustom, calls=%fused_computation.1 | custom fusion | bytes 40960 | tf_op jit(solution)/shard_map/jit(take_along_axis)/gather | solution.py:57
  177.3 0.2 copy.27
  177.5 0.6 select_bitcast_fusion
  (46 shorter events, 2.6 us)
Async XLA Ops:
  6.5 6.0 %sort.19.cloned.1.call-start = ((), (), s32[]{:S(2)}) async-start(), calls=%async_computation | async-start | bytes 24608 | tf_op jit(solution)/shard_map/jit(argsort)/sort | solution.py:56
  7.3 1.7 copy-start
  7.3 2.0 %copy-start.2 = (bf16[4,4,256]{2,1,0:T(4,128)(2,1)S(1)}, bf16[4,4,256]{2,1,0:T(4,128)(2,1)}, u32[]{:S(2)}) copy-start(bf16[4,4,256]{2,1,0:T(4,128)(2,1)} %param.4) | copy-start | bytes 24580
  9.5 3.1 %copy-start.1 = (s32[4,256]{1,0:T(4,128)S(1)}, s32[4,256]{1,0:T(4,128)}, u32[]{:S(2)}) copy-start(s32[4,256]{1,0:T(4,128)} %param.5) | copy-start | bytes 12292
  20.1 4.6 %collective-permute-start = (bf16[4,4,64]{2,1,0:T(4,128)(2,1)S(1)}, bf16[4,4,64]{2,1,0:T(4,128)(2,1)S(1)}, u32[]{:S(2)}, u32[]{:S(2)}) collective-permute-start(bf16[4,4,64]{2,1,0:T(4,128)(2,1)S(1)} %fusion.18), channel_id=1, source_target_pairs={{0,16},{16,0},{4,20},{20,4},{8,24},{24,8},{12,28},{28,12},{1,17},{... | collective-permute-start | bytes 6152 | tf_op jit(solution)/shard_map/ppermute | solution.py:16
  44.3 3.6 %collective-permute-start.1 = (bf16[4,4,64]{2,1,0:T(4,128)(2,1)S(1)}, bf16[4,4,64]{2,1,0:T(4,128)(2,1)S(1)}, u32[]{:S(2)}, u32[]{:S(2)}) collective-permute-start(bf16[4,4,64]{2,1,0:T(4,128)(2,1)S(1)} %dynamic-slice_convert_fusion.6), channel_id=1, source_target_pairs={{0,8},{8,0},{4,12},{12,4},{16,24},{24,16},{20,28},{28,20},{1,9},{9... | collective-permute-start | bytes 6152 | tf_op jit(solution)/shard_map/ppermute | solution.py:16
  63.7 1.2 collective-permute-start.2
  113.9 3.6 %collective-permute-start.3 = (bf16[4,4,64]{2,1,0:T(4,128)(2,1)S(1)}, bf16[4,4,64]{2,1,0:T(4,128)(2,1)S(1)}, u32[]{:S(2)}, u32[]{:S(2)}) collective-permute-start(bf16[4,4,64]{2,1,0:T(4,128)(2,1)S(1)} %dynamic-slice_convert_fusion.2), channel_id=1, source_target_pairs={{0,16},{16,0},{4,20},{20,4},{8,24},{24,8},{12,28},{28,12},{1,17},{... | collective-permute-start | bytes 6152 | tf_op jit(solution)/shard_map/ppermute | solution.py:16
  133.4 3.6 %collective-permute-start.4 = (bf16[4,4,64]{2,1,0:T(4,128)(2,1)S(1)}, bf16[4,4,64]{2,1,0:T(4,128)(2,1)S(1)}, u32[]{:S(2)}, u32[]{:S(2)}) collective-permute-start(bf16[4,4,64]{2,1,0:T(4,128)(2,1)S(1)} %dynamic-slice_convert_fusion.1), channel_id=1, source_target_pairs={{0,8},{8,0},{4,12},{12,4},{16,24},{24,16},{20,28},{28,20},{1,9},{9... | collective-permute-start | bytes 6152 | tf_op jit(solution)/shard_map/ppermute | solution.py:16
  153.4 1.2 collective-permute-start.5
Sparse Core Ops, SparseCore 0:
  9.7 2.5 sort.21.cloned.1.call-done
  (1 shorter events, 0.0 us)
where the time goes:
time: 185 us
  blocking collectives  131 us (71%)
  local copies, waits for them, and re-layouts  19.4 us (10%)
  between operations  13.6 us (7%)
  waiting for transfers between devices  9.36 us (5%)
  starting transfers between devices  7.49 us (4%)
  other arithmetic  2.37 us (1%)
    psum x8, blocking collectives, local(): current = lax.psum(terms, 'rank')  131 us
    ppermute x6, waiting for transfers between devices, swapped(): return lax.ppermute(block, axis, route)  9.36 us
    ppermute x6, starting transfers between devices, swapped(): return lax.ppermute(block, axis, route)  7.49 us
    gather x2, local copies, waits for them, and re-layouts, local(): return jnp.take_along_axis(current, inverse[:, None, :], axis=2)  6.98 us
    gather x2, local copies, waits for them, and re-layouts, local(): jnp.take_along_axis(load_vectors, cluster_order[:, None, :], axis=2)  5.96 us
  transfers between devices with their start and end apart: 6, of which 6 were waited for; matrix products, arithmetic and copies ran while one was open for 0% of the time, Pallas kernels for 0%

commit v1 on v0

v1 whole, which is shorter than its diff:
```python
import functools

import jax
import jax.numpy as jnp
from jax import lax
from jax.experimental import pallas as pl
from jax.experimental.pallas import tpu as pltpu
from jax.sharding import PartitionSpec as P

MESH = pl.DeviceIdType.MESH


def kernel(
    leaves,
    ranks,
    loads_hbm,
    order_hbm,
    present_hbm,
    factors_hbm,
    out_ref,
    loads_ref,
    order_ref,
    present_ref,
    weights,
    last_weights,
    send,
    recv,
    last_send,
    last_recv,
    in_sem,
    weight_sem,
    send_sem,
    recv_sem,
    last_send_sem,
    last_recv_sem,
):
    levels, blocks, _, columns, width = factors_hbm.shape
    loads = loads_hbm.shape[1]
    half = blocks // 2
    rows = half * loads
    lanes = 2 * columns
    local_bits = blocks.bit_length() - 1
    tree_bits = local_bits + leaves.bit_length() - 1
    level_bits = [(tree_bits - 1 - level) % tree_bits for level in range(levels)]
    leaf = lax.axis_index("leaf")
    rank = lax.axis_index("rank")

    def partner_leaf(bit):
        step = 1 << (bit - local_bits)
        return leaf + step - 2 * step * ((leaf // step) % 2)

    def other_rank(away):
        return (rank + away) % ranks

    barrier = pltpu.get_barrier_semaphore()
    remote_bits = sorted({bit for bit in level_bits if bit >= local_bits})
    for away in range(1, ranks):
        pl.semaphore_signal(
            barrier, inc=1, device_id={"leaf": leaf, "rank": other_rank(away)}, device_id_type=MESH
        )
    for bit in remote_bits:
        for away in range(ranks):
            pl.semaphore_signal(
                barrier,
                inc=1,
                device_id={"leaf": partner_leaf(bit), "rank": other_rank(away)},
                device_id_type=MESH,
            )

    fetches = [
        pltpu.make_async_copy(order_hbm, order_ref, in_sem.at[0]),
        pltpu.make_async_copy(loads_hbm, loads_ref, in_sem.at[1]),
        pltpu.make_async_copy(present_hbm, present_ref, in_sem.at[2]),
    ]
    weight_fetches = [
        pltpu.make_async_copy(factors_hbm.at[level], weights.at[level], weight_sem.at[level])
        for level in range(levels)
    ]
    for fetch in fetches + weight_fetches:
        fetch.start()
    for fetch in fetches:
        fetch.wait()

    lane = lax.broadcasted_iota(jnp.int32, (rows, lanes), 1)
    row = lax.broadcasted_iota(jnp.int32, (rows, lanes), 0)
    left = lane < columns

    def picks(block):
        wanted = lax.broadcasted_iota(jnp.int32, (width, width), 0)
        return jnp.where(order_ref[pl.ds(block, 1), :] == wanted, 1.0, 0.0).astype(jnp.bfloat16)

    def gathered(block):
        return jnp.dot(loads_ref[block], picks(block), preferred_element_type=jnp.float32)

    def packed(upper, lower):
        own, partner = [], []
        for tile in range(ranks // 2):
            a = upper[:, tile * lanes : (tile + 1) * lanes]
            b = lower[:, tile * lanes : (tile + 1) * lanes]
            a_moved = pltpu.roll(a, columns, 1)
            b_moved = pltpu.roll(b, columns, 1)
            own += [jnp.where(left, a, b_moved), jnp.where(left, a_moved, b)]
            partner += [jnp.where(left, b, a_moved), jnp.where(left, b_moved, a)]
        return own, partner

    def present_mask(level):
        def rows_of(first):
            mask = jnp.zeros((rows, lanes), jnp.float32)
            for at in range(half):
                value = present_ref[level, first + at].astype(jnp.float32)
                mask = jnp.where(row // loads == at, value, mask)
            return mask

        return jnp.where(left, rows_of(half), rows_of(0))

    def remote(level, src, slot, to_leaf, to_rank):
        return pltpu.make_async_remote_copy(
            src_ref=src,
            dst_ref=recv.at[level, slot],
            send_sem=send_sem.at[level],
            recv_sem=recv_sem.at[level],
            device_id={"leaf": to_leaf, "rank": to_rank},
            device_id_type=MESH,
        )

    sent = [0] * levels

    first = [gathered(block) for block in range(blocks)]
    own, partner = packed(
        jnp.concatenate(first[:half], axis=0), jnp.concatenate(first[half:], axis=0)
    )
    for at in range(ranks):
        send[0, 0, at] = own[at]
        send[0, 1, at] = partner[at]
    pl.semaphore_wait(barrier, ranks - 1 + len(remote_bits) * ranks)
    if level_bits[0] >= local_bits:
        remote(0, send.at[0, 1, rank], ranks, partner_leaf(level_bits[0]), rank).start()
        sent[0] = 1

    for level in range(levels):
        bit = level_bits[level]
        mask = present_mask(level)
        if level == min(1, levels - 1):
            weight_fetches[levels - 1].wait()
            for block in range(blocks):
                wanted = picks(block)
                for side in range(2):
                    last_weights[block, side] = lax.dot_general(
                        weights[levels - 1, block, side],
                        wanted,
                        (((1,), (1,)), ((), ())),
                        preferred_element_type=jnp.float32,
                    ).astype(jnp.bfloat16)
        if level < levels - 1:
            weight_fetches[level].wait()
        if sent[level]:
            arrived = recv.at[level, pl.ds(0, sent[level])]
            pltpu.make_async_copy(arrived, arrived, recv_sem.at[level]).wait()
        if level == 0:
            state = send[0, 0, rank]
        else:
            state = recv[level, 0]
            for at in range(1, ranks):
                state = state + recv[level, at]
        if bit >= local_bits:
            other = recv[level, ranks]
            if level > 0:
                for at in range(1, ranks):
                    other = other + recv[level, ranks + at]
        elif bit == local_bits - 1:
            other = state
        else:
            away = loads << bit
            moved = pltpu.roll(state, columns, 1)
            other = jnp.where(
                (row // away) % 2 == 0,
                pltpu.roll(moved, rows - away, 0),
                pltpu.roll(moved, away, 0),
            )
        other = other * mask
        upper = jnp.where(left, state, other)
        lower = jnp.where(left, other, state)

        def spread(piece):
            return jnp.concatenate(
                [jnp.where(row // loads == at, piece, 0.0) for at in range(half)], axis=1
            ).astype(jnp.bfloat16)

        table = weights.at[level] if level < levels - 1 else last_weights
        upper_weights = [table[at, side] for at in range(half) for side in (0, 1)]
        lower_weights = [table[half + at, side] for at in range(half) for side in (1, 0)]
        upper = jnp.dot(
            spread(upper),
            jnp.concatenate(upper_weights, axis=0),
            preferred_element_type=jnp.float32,
        )
        lower = jnp.dot(
            spread(lower),
            jnp.concatenate(lower_weights, axis=0),
            preferred_element_type=jnp.float32,
        )
        if level == levels - 1:
            break
        own, partner = packed(upper, lower)
        then = level + 1
        with_partner = level_bits[then] >= local_bits
        for at in range(ranks):
            send[then, 0, at] = own[at]
            if with_partner:
                send[then, 1, at] = partner[at]
        for away in range(1, ranks):
            to = other_rank(away)
            remote(then, send.at[then, 0, to], rank, leaf, to).start()
            if with_partner:
                remote(
                    then, send.at[then, 1, to], ranks + rank, partner_leaf(level_bits[then]), to
                ).start()
        if with_partner:
            remote(
                then, send.at[then, 1, rank], ranks + rank, partner_leaf(level_bits[then]), rank
            ).start()
        sent[then] = ranks - 1 + (ranks if with_partner else 0)
        recv[then, rank] = send[then, 0, rank]

    last_send[...] = jnp.concatenate([upper, lower], axis=0).astype(jnp.bfloat16)
    lasts = [
        pltpu.make_async_remote_copy(
            src_ref=last_send,
            dst_ref=last_recv.at[rank],
            send_sem=last_send_sem,
            recv_sem=last_recv_sem,
            device_id={"leaf": leaf, "rank": other_rank(away)},
            device_id_type=MESH,
        )
        for away in range(1, ranks)
    ]
    for copy in lasts:
        copy.start()
    last_recv[rank] = last_send[...]
    for level in range(levels):
        if sent[level]:
            gone = recv.at[level, pl.ds(0, sent[level])]
            pltpu.make_async_copy(gone, gone, send_sem.at[level]).wait()
    arrived = last_recv.at[pl.ds(0, ranks - 1)]
    pltpu.make_async_copy(arrived, arrived, last_recv_sem).wait()
    total = last_recv[0].astype(jnp.float32)
    for at in range(1, ranks):
        total = total + last_recv[at].astype(jnp.float32)
    for block in range(blocks):
        out_ref[block] = total[block * loads : (block + 1) * loads]
    pltpu.make_async_copy(arrived, arrived, last_send_sem).wait()


def local(leaves, ranks, load_vectors, cluster_order, block_present, factors):
    levels, blocks, _, columns, width = factors.shape
    loads = load_vectors.shape[1]
    rows = blocks // 2 * loads
    lanes = 2 * columns
    return pl.pallas_call(
        functools.partial(kernel, leaves, ranks),
        out_shape=jax.ShapeDtypeStruct((blocks, loads, width), jnp.float32),
        in_specs=[pl.BlockSpec(memory_space=pl.ANY)] * 4,
        out_specs=pl.BlockSpec(memory_space=pltpu.VMEM),
        scratch_shapes=[
            pltpu.VMEM(load_vectors.shape, load_vectors.dtype),
            pltpu.VMEM(cluster_order.shape, cluster_order.dtype),
            pltpu.SMEM(block_present.shape, block_present.dtype),
            pltpu.VMEM(factors.shape, factors.dtype),
            pltpu.VMEM(factors.shape[1:], factors.dtype),
            pltpu.VMEM((levels, 2, ranks, rows, lanes), jnp.float32),
            pltpu.VMEM((levels, 2 * ranks, rows, lanes), jnp.float32),
            pltpu.VMEM((blocks * loads, width), jnp.bfloat16),
            pltpu.VMEM((ranks, blocks * loads, width), jnp.bfloat16),
            pltpu.SemaphoreType.DMA((3,)),
            pltpu.SemaphoreType.DMA((levels,)),
            pltpu.SemaphoreType.DMA((levels,)),
            pltpu.SemaphoreType.DMA((levels,)),
            pltpu.SemaphoreType.DMA,
            pltpu.SemaphoreType.DMA,
        ],
        compiler_params=pltpu.CompilerParams(
            collective_id=0, has_side_effects=True, vmem_limit_bytes=32 * 1024 * 1024
        ),
    )(load_vectors, cluster_order, block_present, factors)


def solution(mesh):
    in_specs = (
        P("leaf", None, None),
        P("leaf", None),
        P(None, "leaf"),
        P(None, "leaf", None, "rank", None),
    )
    return jax.shard_map(
        functools.partial(local, mesh.shape["leaf"], mesh.shape["rank"]),
        mesh=mesh,
        in_specs=in_specs,
        out_specs=P("leaf", None, None),
        check_vma=False,
    )
```

time: 185 us -> 45.4 us (0.25)
  blocking collectives: 131 us -> 0 us
  Pallas kernels: 0 us -> 40.7 us
  local copies, waits for them, and re-layouts: 19.4 us -> 4.34 us
  between operations: 13.6 us -> 0.01 us
  waiting for transfers between devices: 9.36 us -> 0 us
  starting transfers between devices: 7.49 us -> 0 us
  other arithmetic: 2.37 us -> 0 us
    psum x8 -> x0, blocking collectives: 131 us -> none  [local(): current = lax.psum(terms, 'rank')]
    pallas_call x0 -> x1, Pallas kernels: none -> 40.7 us  [local(): pl.pallas_call(functools.partial(kernel, leaves, ranks), out_shape=jax.Sh...]
    gather x4 -> x0, local copies, waits for them, and re-layouts: 12.9 us -> none  [the longest x2 6.98 us: local(): return jnp.take_along_axis(current, inverse[:, None, :], axis=2)]
    ppermute x6 -> x0, waiting for transfers between devices: 9.36 us -> none  [swapped(): return lax.ppermute(block, axis, route)]
    ppermute x6 -> x0, starting transfers between devices: 7.49 us -> none  [swapped(): return lax.ppermute(block, axis, route)]
    unnamed x19 -> x8, local copies, waits for them, and re-layouts: 0.58 us -> 4.34 us
    sort x2 -> x0, local copies, waits for them, and re-layouts: 2.87 us -> none  [local(): inverse = jnp.argsort(cluster_order, axis=1)]
  transfers between devices with their start and end apart: 6 -> 0, of which waited for: 6 -> 0; matrix products, arithmetic and copies ran while one was open for 0% -> 0% of each run, Pallas kernels for 0% -> 0%
where the time goes in v1:
time: 45.4 us; the launch traced here: 45.1 us
  Pallas kernels  40.7 us (90%)
  local copies, waits for them, and re-layouts  4.34 us (10%)
    pallas_call x1, Pallas kernels, local(): pl.pallas_call(functools.partial(kernel, leaves, ranks), out_shape=jax.Sh...  40.7 us
    unnamed x8, local copies, waits for them, and re-layouts  4.34 us

profile of v1, /device:TPU:0, one launch (start us, length us, event | category | flops | bytes accessed | tf_op | source)
XLA Modules:
  0.0 45.1 jit_solution(18157701873445904496)
XLA Ops:
  0.0 0.8 %copy.5.present_hbm = s32[8,4]{1,0:T(8,128)S(1)} copy(s32[8,4]{0,1:T(4,128)} %param.6) | data formatting | bytes 256 | tf_op args[2]
  0.8 0.0 copy-start
  0.8 1.6 %copy-done = bf16[8,4,2,64,256]{4,3,2,1,0:T(8,128)(2,1)S(1)} copy-done((bf16[8,4,2,64,256]{4,3,2,1,0:T(8,128)(2,1)S(1)}, bf16[8,4,2,64,256]{4,3,2,1,0:T(8,128)(2,1)}, u32[]{:S(2)}) %copy-start) | copy-done | bytes 2097176
  2.3 0.0 copy-start.1
  2.4 0.7 %copy-done.1 = bf16[4,4,256]{2,1,0:T(4,128)(2,1)S(1)} copy-done((bf16[4,4,256]{2,1,0:T(4,128)(2,1)S(1)}, bf16[4,4,256]{2,1,0:T(4,128)(2,1)}, u32[]{:S(2)}) %copy-start.1) | copy-done | bytes 8216
  3.0 0.0 copy-start.2
  3.0 0.7 %copy-done.2 = s32[4,256]{1,0:T(4,128)S(1)} copy-done((s32[4,256]{1,0:T(4,128)S(1)}, s32[4,256]{1,0:T(4,128)}, u32[]{:S(2)}) %copy-start.2) | copy-done | bytes 4120
  3.7 40.7 %shard_map.46 = f32[4,4,256]{2,1,0:T(4,128)S(1)} custom-call(bf16[4,4,256]{2,1,0:T(4,128)(2,1)S(1)} %copy-done.1, s32[4,256]{1,0:T(4,128)S(1)} %copy-done.2, s32[8,4]{1,0:T(8,128)S(1)} %copy.5.present_hbm, bf16[8,4,2,64,256]{4,3,2,1,0:T(8,128)(2,1)S(1)} %copy-done), custom_call_target="tpu_custom_call" | custom-call | tf_op jit(solution)/shard_map/pallas_call | solution.py:259
  44.5 0.6 %copy.7 = f32[4,4,256]{2,1,0:T(4,128)} copy(f32[4,4,256]{2,1,0:T(4,128)S(1)} %shard_map.46) | data formatting | bytes 32768
Async XLA Ops:
  0.8 1.6 %copy-start = (bf16[8,4,2,64,256]{4,3,2,1,0:T(8,128)(2,1)S(1)}, bf16[8,4,2,64,256]{4,3,2,1,0:T(8,128)(2,1)}, u32[]{:S(2)}) copy-start(bf16[8,4,2,64,256]{4,3,2,1,0:T(8,128)(2,1)} %factors_hbm.1) | copy-start | bytes 6291460
  2.3 0.7 %copy-start.1 = (bf16[4,4,256]{2,1,0:T(4,128)(2,1)S(1)}, bf16[4,4,256]{2,1,0:T(4,128)(2,1)}, u32[]{:S(2)}) copy-start(bf16[4,4,256]{2,1,0:T(4,128)(2,1)} %loads_hbm.1) | copy-start | bytes 24580
  3.0 0.7 %copy-start.2 = (s32[4,256]{1,0:T(4,128)S(1)}, s32[4,256]{1,0:T(4,128)}, u32[]{:S(2)}) copy-start(s32[4,256]{1,0:T(4,128)} %order_hbm.1) | copy-start | bytes 12292

commit v2 on v1

--- a/solution.py
+++ b/solution.py
@@ -8,6 +8,14 @@
 from jax.sharding import PartitionSpec as P
 
 MESH = pl.DeviceIdType.MESH
+VMEM_LIMIT = 63 * 1024 * 1024
+
+
+def whole_level(level_bits, local_bits):
+    for level in range(1, len(level_bits) - 2):
+        if level_bits[level] == local_bits - 1 and level_bits[level + 1] < local_bits:
+            return level
+    return -1
 
 
 def kernel(
@@ -27,12 +35,18 @@
     recv,
     last_send,
     last_recv,
+    whole_send,
+    whole_recv,
+    bulk_send,
+    bulk_recv,
     in_sem,
     weight_sem,
     send_sem,
     recv_sem,
     last_send_sem,
     last_recv_sem,
+    whole_sem,
+    bulk_sem,
 ):
     levels, blocks, _, columns, width = factors_hbm.shape
     loads = loads_hbm.shape[1]
@@ -42,6 +56,7 @@
     local_bits = blocks.bit_length() - 1
     tree_bits = local_bits + leaves.bit_length() - 1
     level_bits = [(tree_bits - 1 - level) % tree_bits for level in range(levels)]
+    whole = whole_level(level_bits, local_bits)
     leaf = lax.axis_index("leaf")
     rank = lax.axis_index("rank")
 
@@ -76,7 +91,8 @@
         pltpu.make_async_copy(factors_hbm.at[level], weights.at[level], weight_sem.at[level])
         for level in range(levels)
     ]
-    for fetch in fetches + weight_fetches:
+    order_of_use = ([whole] if whole > 0 else []) + [level for level in range(levels) if level != whole]
+    for fetch in fetches + [weight_fetches[level] for level in order_of_use]:
         fetch.start()
     for fetch in fetches:
         fetch.wait()
@@ -93,6 +109,7 @@
         return jnp.dot(loads_ref[block], picks(block), preferred_element_type=jnp.float32)
 
     def packed(upper, lower):
+        left = lax.broadcasted_iota(jnp.int32, (upper.shape[0], lanes), 1) < columns
         own, partner = [], []
         for tile in range(ranks // 2):
             a = upper[:, tile * lanes : (tile + 1) * lanes]
@@ -107,7 +124,7 @@
         def rows_of(first):
             mask = jnp.zeros((rows, lanes), jnp.float32)
             for at in range(half):
-                value = present_ref[level, first + at].astype(jnp.float32)
+                value = present_ref[first + at, level].astype(jnp.float32)
                 mask = jnp.where(row // loads == at, value, mask)
             return mask
 
@@ -132,13 +149,66 @@
     for at in range(ranks):
         send[0, 0, at] = own[at]
         send[0, 1, at] = partner[at]
+    bulk = []
+    if whole > 0:
+        weight_fetches[whole].wait()
+        for at in range(half):
+            for side in range(2):
+                pieces, _ = packed(
+                    weights[whole, at, side].astype(jnp.float32),
+                    weights[whole, half + at, side].astype(jnp.float32),
+                )
+                for to in range(ranks):
+                    bulk_send[to, at, side] = pieces[to].astype(jnp.bfloat16)
+        bulk_recv[rank] = bulk_send[rank]
+        for away in range(1, ranks):
+            bulk.append(
+                pltpu.make_async_remote_copy(
+                    src_ref=bulk_send.at[other_rank(away)],
+                    dst_ref=bulk_recv.at[rank],
+                    send_sem=bulk_sem.at[0],
+                    recv_sem=bulk_sem.at[1],
+                    device_id={"leaf": leaf, "rank": other_rank(away)},
+                    device_id_type=MESH,
+                )
+            )
     pl.semaphore_wait(barrier, ranks - 1 + len(remote_bits) * ranks)
     if level_bits[0] >= local_bits:
         remote(0, send.at[0, 1, rank], ranks, partner_leaf(level_bits[0]), rank).start()
         sent[0] = 1
+    for copy in bulk if whole == 1 else []:
+        copy.start()
 
     for level in range(levels):
         bit = level_bits[level]
+        if level == whole:
+            all_rows = (blocks * loads, width)
+            block_at = lax.broadcasted_iota(jnp.int32, all_rows, 0) // loads
+            mask = jnp.zeros(all_rows, jnp.float32)
+            for block in range(blocks):
+                mask = jnp.where(
+                    block_at == block, present_ref[block, level].astype(jnp.float32), mask
+                )
+            arrived = bulk_recv.at[pl.ds(0, ranks - 1)]
+            pltpu.make_async_copy(arrived, arrived, bulk_sem.at[1]).wait()
+            arrived = whole_recv.at[pl.ds(0, ranks - 1)]
+            pltpu.make_async_copy(arrived, arrived, whole_sem.at[1]).wait()
+            total = whole_recv[0].astype(jnp.float32)
+            for at in range(1, ranks):
+                total = total + whole_recv[at].astype(jnp.float32)
+            other = jnp.concatenate([total[rows:], total[:rows]], axis=0) * mask
+            spans, table = [], []
+            for at in range(half):
+                for side, value in enumerate((total, other)):
+                    spans.append(jnp.where(block_at % half == at, value, 0.0).astype(jnp.bfloat16))
+                    table += [bulk_recv[source, at, side] for source in range(ranks)]
+            both = jnp.dot(
+                jnp.concatenate(spans, axis=1),
+                jnp.concatenate(table, axis=0),
+                preferred_element_type=jnp.float32,
+            )
+            carried = jnp.where(left, both[:rows], both[rows:])
+            continue
         mask = present_mask(level)
         if level == min(1, levels - 1):
             weight_fetches[levels - 1].wait()
@@ -158,6 +228,8 @@
             pltpu.make_async_copy(arrived, arrived, recv_sem.at[level]).wait()
         if level == 0:
             state = send[0, 0, rank]
+        elif level - 1 == whole:
+            state = carried
         else:
             state = recv[level, 0]
             for at in range(1, ranks):
@@ -201,8 +273,21 @@
         )
         if level == levels - 1:
             break
+        then = level + 1
+        if then == whole:
+            whole_send[...] = jnp.concatenate([upper, lower], axis=0).astype(jnp.bfloat16)
+            for away in range(1, ranks):
+                pltpu.make_async_remote_copy(
+                    src_ref=whole_send,
+                    dst_ref=whole_recv.at[rank],
+                    send_sem=whole_sem.at[0],
+                    recv_sem=whole_sem.at[1],
+                    device_id={"leaf": leaf, "rank": other_rank(away)},
+                    device_id_type=MESH,
+                ).start()
+            whole_recv[rank] = whole_send[...]
+            continue
         own, partner = packed(upper, lower)
-        then = level + 1
         with_partner = level_bits[then] >= local_bits
         for at in range(ranks):
             send[then, 0, at] = own[at]
@@ -220,6 +305,8 @@
                 then, send.at[then, 1, rank], ranks + rank, partner_leaf(level_bits[then]), rank
             ).start()
         sent[then] = ranks - 1 + (ranks if with_partner else 0)
+        for copy in bulk if then == whole - 1 else []:
+            copy.start()
         recv[then, rank] = send[then, 0, rank]
 
     last_send[...] = jnp.concatenate([upper, lower], axis=0).astype(jnp.bfloat16)
@@ -241,6 +328,11 @@
         if sent[level]:
             gone = recv.at[level, pl.ds(0, sent[level])]
             pltpu.make_async_copy(gone, gone, send_sem.at[level]).wait()
+    if whole > 0:
+        gone = bulk_recv.at[pl.ds(0, ranks - 1)]
+        pltpu.make_async_copy(gone, gone, bulk_sem.at[0]).wait()
+        gone = whole_recv.at[pl.ds(0, ranks - 1)]
+        pltpu.make_async_copy(gone, gone, whole_sem.at[0]).wait()
     arrived = last_recv.at[pl.ds(0, ranks - 1)]
     pltpu.make_async_copy(arrived, arrived, last_recv_sem).wait()
     total = last_recv[0].astype(jnp.float32)
@@ -264,24 +356,30 @@
         scratch_shapes=[
             pltpu.VMEM(load_vectors.shape, load_vectors.dtype),
             pltpu.VMEM(cluster_order.shape, cluster_order.dtype),
-            pltpu.SMEM(block_present.shape, block_present.dtype),
+            pltpu.SMEM(block_present.shape[::-1], block_present.dtype),
             pltpu.VMEM(factors.shape, factors.dtype),
             pltpu.VMEM(factors.shape[1:], factors.dtype),
             pltpu.VMEM((levels, 2, ranks, rows, lanes), jnp.float32),
             pltpu.VMEM((levels, 2 * ranks, rows, lanes), jnp.float32),
             pltpu.VMEM((blocks * loads, width), jnp.bfloat16),
             pltpu.VMEM((ranks, blocks * loads, width), jnp.bfloat16),
+            pltpu.VMEM((blocks * loads, width), jnp.bfloat16),
+            pltpu.VMEM((ranks, blocks * loads, width), jnp.bfloat16),
+            pltpu.VMEM((ranks, blocks // 2, 2, columns, lanes), factors.dtype),
+            pltpu.VMEM((ranks, blocks // 2, 2, columns, lanes), factors.dtype),
             pltpu.SemaphoreType.DMA((3,)),
             pltpu.SemaphoreType.DMA((levels,)),
             pltpu.SemaphoreType.DMA((levels,)),
             pltpu.SemaphoreType.DMA((levels,)),
             pltpu.SemaphoreType.DMA,
             pltpu.SemaphoreType.DMA,
+            pltpu.SemaphoreType.DMA((2,)),
+            pltpu.SemaphoreType.DMA((2,)),
         ],
         compiler_params=pltpu.CompilerParams(
-            collective_id=0, has_side_effects=True, vmem_limit_bytes=32 * 1024 * 1024
+            collective_id=0, has_side_effects=True, vmem_limit_bytes=VMEM_LIMIT
         ),
-    )(load_vectors, cluster_order, block_present, factors)
+    )(load_vectors, cluster_order, block_present.T, factors)
 
 
 def solution(mesh):

time: 45.4 us -> 38.9 us (0.86)
  Pallas kernels: 40.7 us -> 37.3 us
  local copies, waits for them, and re-layouts: 4.34 us -> 1.32 us
    pallas_call x1, Pallas kernels: 40.7 us -> 37.3 us  [local(): pl.pallas_call(functools.partial(kernel, leaves, ranks), out_shape=jax.Sh...]
    unnamed x8 -> x1, local copies, waits for them, and re-layouts: 4.34 us -> 1.32 us
where the time goes in v2:
time: 38.9 us; the launch traced here: 38.6 us
  Pallas kernels  37.3 us (96%)
  local copies, waits for them, and re-layouts  1.32 us (3%)
    pallas_call x1, Pallas kernels, local(): pl.pallas_call(functools.partial(kernel, leaves, ranks), out_shape=jax.Sh...  37.3 us
    unnamed x1, local copies, waits for them, and re-layouts  1.32 us

profile of v2, /device:TPU:0, one launch (start us, length us, event | category | flops | bytes accessed | tf_op | source)
XLA Modules:
  0.0 38.6 jit_solution(15194610350596069339)
XLA Ops:
  0.0 37.3 %shard_map.46 = f32[4,4,256]{2,1,0:T(4,128)} custom-call(bf16[4,4,256]{2,1,0:T(4,128)(2,1)} %loads_hbm.1, s32[4,256]{1,0:T(4,128)} %order_hbm.1, s32[4,8]{1,0:T(4,128)} %bitcast.1, bf16[8,4,2,64,256]{4,3,2,1,0:T(8,128)(2,1)} %factors_hbm.1), custom_call_target="tpu_custom_call" | custom-call | tf_op jit(solution)/shard_map/pallas_call | solution.py:351
  37.3 1.3 %copy.6 = f32[4,4,256]{2,1,0:T(4,128)} copy(f32[4,4,256]{2,1,0:T(4,128)} %shard_map.46) | data formatting | bytes 32768

commit v3 on v1

--- a/solution.py
+++ b/solution.py
@@ -8,6 +8,17 @@
 from jax.sharding import PartitionSpec as P
 
 MESH = pl.DeviceIdType.MESH
+BULK_LEAD = 2
+VMEM_LIMIT = 63 * 1024 * 1024
+
+
+def whole_levels(level_bits, local_bits):
+    chosen = []
+    for level in range(3, len(level_bits) - 1):
+        near = level_bits[level + 1] <= local_bits and level_bits[level] >= local_bits - 1
+        if near and level - 1 not in chosen:
+            chosen.append(level)
+    return chosen
 
 
 def kernel(
@@ -27,12 +38,18 @@
     recv,
     last_send,
     last_recv,
+    whole_send,
+    whole_recv,
+    bulk_send,
+    bulk_recv,
     in_sem,
     weight_sem,
     send_sem,
     recv_sem,
     last_send_sem,
     last_recv_sem,
+    whole_sem,
+    bulk_sem,
 ):
     levels, blocks, _, columns, width = factors_hbm.shape
     loads = loads_hbm.shape[1]
@@ -42,6 +59,8 @@
     local_bits = blocks.bit_length() - 1
     tree_bits = local_bits + leaves.bit_length() - 1
     level_bits = [(tree_bits - 1 - level) % tree_bits for level in range(levels)]
+    wholes = whole_levels(level_bits, local_bits)
+    rounds = [level for level in range(1, levels) if level - 1 not in wholes]
     leaf = lax.axis_index("leaf")
     rank = lax.axis_index("rank")
 
@@ -76,7 +95,8 @@
         pltpu.make_async_copy(factors_hbm.at[level], weights.at[level], weight_sem.at[level])
         for level in range(levels)
     ]
-    for fetch in fetches + weight_fetches:
+    order_of_use = wholes[:1] + [level for level in range(levels) if level not in wholes[:1]]
+    for fetch in fetches + [weight_fetches[level] for level in order_of_use]:
         fetch.start()
     for fetch in fetches:
         fetch.wait()
@@ -93,6 +113,7 @@
         return jnp.dot(loads_ref[block], picks(block), preferred_element_type=jnp.float32)
 
     def packed(upper, lower):
+        left = lax.broadcasted_iota(jnp.int32, (upper.shape[0], lanes), 1) < columns
         own, partner = [], []
         for tile in range(ranks // 2):
             a = upper[:, tile * lanes : (tile + 1) * lanes]
@@ -107,7 +128,7 @@
         def rows_of(first):
             mask = jnp.zeros((rows, lanes), jnp.float32)
             for at in range(half):
-                value = present_ref[level, first + at].astype(jnp.float32)
+                value = present_ref[first + at, level].astype(jnp.float32)
                 mask = jnp.where(row // loads == at, value, mask)
             return mask
 
@@ -132,13 +153,90 @@
     for at in range(ranks):
         send[0, 0, at] = own[at]
         send[0, 1, at] = partner[at]
+    bulk = {level: [] for level in range(levels)}
+
+    def prepare_bulk(at_whole):
+        level = wholes[at_whole]
+        weight_fetches[level].wait()
+        before = rounds[: rounds.index(level)]
+        for at in range(half):
+            for side in range(2):
+                pieces, _ = packed(
+                    weights[level, at, side].astype(jnp.float32),
+                    weights[level, half + at, side].astype(jnp.float32),
+                )
+                for to in range(ranks):
+                    bulk_send[at_whole, to, at, side] = pieces[to].astype(jnp.bfloat16)
+            for away in range(1, ranks):
+                to = other_rank(away)
+                bulk[before[max(at - BULK_LEAD, -len(before))]].append(
+                    pltpu.make_async_remote_copy(
+                        src_ref=bulk_send.at[at_whole, to, at],
+                        dst_ref=bulk_recv.at[at_whole, rank, at],
+                        send_sem=bulk_sem.at[at_whole, 0],
+                        recv_sem=bulk_sem.at[at_whole, 1],
+                        device_id={"leaf": leaf, "rank": to},
+                        device_id_type=MESH,
+                    )
+                )
+        bulk_recv[at_whole, rank] = bulk_send[at_whole, rank]
+
+    for at_whole in range(len(wholes[:1])):
+        prepare_bulk(at_whole)
     pl.semaphore_wait(barrier, ranks - 1 + len(remote_bits) * ranks)
     if level_bits[0] >= local_bits:
         remote(0, send.at[0, 1, rank], ranks, partner_leaf(level_bits[0]), rank).start()
         sent[0] = 1
+    for at_whole in range(1, len(wholes)):
+        prepare_bulk(at_whole)
 
     for level in range(levels):
         bit = level_bits[level]
+        if level in wholes:
+            at_whole = wholes.index(level)
+            all_rows = (blocks * loads, width)
+            block_at = lax.broadcasted_iota(jnp.int32, all_rows, 0) // loads
+            mask = jnp.zeros(all_rows, jnp.float32)
+            for block in range(blocks):
+                mask = jnp.where(
+                    block_at == block, present_ref[block, level].astype(jnp.float32), mask
+                )
+            arrived = bulk_recv.at[at_whole, pl.ds(0, ranks - 1)]
+            pltpu.make_async_copy(arrived, arrived, bulk_sem.at[at_whole, 1]).wait()
+            arrived = whole_recv.at[at_whole, pl.ds(0, sent[level])]
+            pltpu.make_async_copy(arrived, arrived, whole_sem.at[at_whole, 1]).wait()
+
+            def summed(first):
+                result = whole_recv[at_whole, first].astype(jnp.float32)
+                for at in range(1, ranks):
+                    result = result + whole_recv[at_whole, first + at].astype(jnp.float32)
+                return result
+
+            total = summed(0)
+            if bit >= local_bits:
+                other = summed(ranks)
+            else:
+                other = jnp.concatenate([total[rows:], total[:rows]], axis=0)
+            other = other * mask
+            spans, table = [], []
+            for at in range(half):
+                for side, value in enumerate((total, other)):
+                    spans.append(jnp.where(block_at % half == at, value, 0.0).astype(jnp.bfloat16))
+                    table += [bulk_recv[at_whole, source, at, side] for source in range(ranks)]
+            both = jnp.dot(
+                jnp.concatenate(spans, axis=1),
+                jnp.concatenate(table, axis=0),
+                preferred_element_type=jnp.float32,
+            )
+            carried = jnp.where(left, both[:rows], both[rows:])
+            then = level + 1
+            if level_bits[then] >= local_bits:
+                send[then, 1, 0] = pltpu.roll(carried, columns, 1)
+                remote(
+                    then, send.at[then, 1, 0], ranks, partner_leaf(level_bits[then]), rank
+                ).start()
+                sent[then] = 1
+            continue
         mask = present_mask(level)
         if level == min(1, levels - 1):
             weight_fetches[levels - 1].wait()
@@ -158,13 +256,15 @@
             pltpu.make_async_copy(arrived, arrived, recv_sem.at[level]).wait()
         if level == 0:
             state = send[0, 0, rank]
+        elif level - 1 in wholes:
+            state = carried
         else:
             state = recv[level, 0]
             for at in range(1, ranks):
                 state = state + recv[level, at]
         if bit >= local_bits:
             other = recv[level, ranks]
-            if level > 0:
+            if level > 0 and level - 1 not in wholes:
                 for at in range(1, ranks):
                     other = other + recv[level, ranks + at]
         elif bit == local_bits - 1:
@@ -201,9 +301,36 @@
         )
         if level == levels - 1:
             break
-        own, partner = packed(upper, lower)
         then = level + 1
         with_partner = level_bits[then] >= local_bits
+        sent[then] = ranks - 1 + (ranks if with_partner else 0)
+        if then in wholes:
+            at_whole = wholes.index(then)
+            whole_send[at_whole] = jnp.concatenate([upper, lower], axis=0).astype(jnp.bfloat16)
+
+            def send_whole(slot, to_leaf, to_rank):
+                pltpu.make_async_remote_copy(
+                    src_ref=whole_send.at[at_whole],
+                    dst_ref=whole_recv.at[at_whole, slot],
+                    send_sem=whole_sem.at[at_whole, 0],
+                    recv_sem=whole_sem.at[at_whole, 1],
+                    device_id={"leaf": to_leaf, "rank": to_rank},
+                    device_id_type=MESH,
+                ).start()
+
+            for away in range(1, ranks):
+                send_whole(rank, leaf, other_rank(away))
+                if with_partner:
+                    send_whole(
+                        ranks + rank, partner_leaf(level_bits[then]), other_rank(away)
+                    )
+            if with_partner:
+                send_whole(ranks + rank, partner_leaf(level_bits[then]), rank)
+            for copy in bulk[then]:
+                copy.start()
+            whole_recv[at_whole, rank] = whole_send[at_whole]
+            continue
+        own, partner = packed(upper, lower)
         for at in range(ranks):
             send[then, 0, at] = own[at]
             if with_partner:
@@ -219,7 +346,8 @@
             remote(
                 then, send.at[then, 1, rank], ranks + rank, partner_leaf(level_bits[then]), rank
             ).start()
-        sent[then] = ranks - 1 + (ranks if with_partner else 0)
+        for copy in bulk[then]:
+            copy.start()
         recv[then, rank] = send[then, 0, rank]
 
     last_send[...] = jnp.concatenate([upper, lower], axis=0).astype(jnp.bfloat16)
@@ -238,9 +366,14 @@
         copy.start()
     last_recv[rank] = last_send[...]
     for level in range(levels):
-        if sent[level]:
+        if sent[level] and level not in wholes:
             gone = recv.at[level, pl.ds(0, sent[level])]
             pltpu.make_async_copy(gone, gone, send_sem.at[level]).wait()
+    for at_whole, level in enumerate(wholes):
+        gone = bulk_recv.at[at_whole, pl.ds(0, ranks - 1)]
+        pltpu.make_async_copy(gone, gone, bulk_sem.at[at_whole, 0]).wait()
+        gone = whole_recv.at[at_whole, pl.ds(0, sent[level])]
+        pltpu.make_async_copy(gone, gone, whole_sem.at[at_whole, 0]).wait()
     arrived = last_recv.at[pl.ds(0, ranks - 1)]
     pltpu.make_async_copy(arrived, arrived, last_recv_sem).wait()
     total = last_recv[0].astype(jnp.float32)
@@ -258,30 +391,36 @@
     lanes = 2 * columns
     return pl.pallas_call(
         functools.partial(kernel, leaves, ranks),
-        out_shape=jax.ShapeDtypeStruct((blocks, loads, width), jnp.float32),
+        out_shape=pltpu.VMEM((blocks, loads, width), jnp.float32),
         in_specs=[pl.BlockSpec(memory_space=pl.ANY)] * 4,
         out_specs=pl.BlockSpec(memory_space=pltpu.VMEM),
         scratch_shapes=[
             pltpu.VMEM(load_vectors.shape, load_vectors.dtype),
             pltpu.VMEM(cluster_order.shape, cluster_order.dtype),
-            pltpu.SMEM(block_present.shape, block_present.dtype),
+            pltpu.SMEM(block_present.shape[::-1], block_present.dtype),
             pltpu.VMEM(factors.shape, factors.dtype),
             pltpu.VMEM(factors.shape[1:], factors.dtype),
             pltpu.VMEM((levels, 2, ranks, rows, lanes), jnp.float32),
             pltpu.VMEM((levels, 2 * ranks, rows, lanes), jnp.float32),
             pltpu.VMEM((blocks * loads, width), jnp.bfloat16),
             pltpu.VMEM((ranks, blocks * loads, width), jnp.bfloat16),
+            pltpu.VMEM((levels, blocks * loads, width), jnp.bfloat16),
+            pltpu.VMEM((levels, 2 * ranks, blocks * loads, width), jnp.bfloat16),
+            pltpu.VMEM((levels, ranks, blocks // 2, 2, columns, lanes), factors.dtype),
+            pltpu.VMEM((levels, ranks, blocks // 2, 2, columns, lanes), factors.dtype),
             pltpu.SemaphoreType.DMA((3,)),
             pltpu.SemaphoreType.DMA((levels,)),
             pltpu.SemaphoreType.DMA((levels,)),
             pltpu.SemaphoreType.DMA((levels,)),
             pltpu.SemaphoreType.DMA,
             pltpu.SemaphoreType.DMA,
+            pltpu.SemaphoreType.DMA((levels, 2)),
+            pltpu.SemaphoreType.DMA((levels, 2)),
         ],
         compiler_params=pltpu.CompilerParams(
-            collective_id=0, has_side_effects=True, vmem_limit_bytes=32 * 1024 * 1024
+            collective_id=0, has_side_effects=True, vmem_limit_bytes=VMEM_LIMIT
         ),
-    )(load_vectors, cluster_order, block_present, factors)
+    )(load_vectors, cluster_order, block_present.T, factors)
 
 
 def solution(mesh):

time: 45.4 us -> 35.3 us (0.78)
  Pallas kernels: 40.7 us -> 34.6 us
  local copies, waits for them, and re-layouts: 4.34 us -> 0.61 us
    pallas_call x1, Pallas kernels: 40.7 us -> 34.6 us  [local(): pl.pallas_call(functools.partial(kernel, leaves, ranks), out_shape=pltpu....]
    unnamed x8 -> x1, local copies, waits for them, and re-layouts: 4.34 us -> 0.61 us
where the time goes in v3:
time: 35.3 us; the launch traced here: 35.2 us
  Pallas kernels  34.6 us (98%)
  local copies, waits for them, and re-layouts  0.61 us (2%)
    pallas_call x1, Pallas kernels, local(): pl.pallas_call(functools.partial(kernel, leaves, ranks), out_shape=pltpu....  34.6 us

profile of v3, /device:TPU:0, one launch (start us, length us, event | category | flops | bytes accessed | tf_op | source)
XLA Modules:
  0.0 35.2 jit_solution(10051471538008594935)
XLA Ops:
  0.0 34.6 %shard_map.46 = f32[4,4,256]{2,1,0:T(4,128)S(1)} custom-call(bf16[4,4,256]{2,1,0:T(4,128)(2,1)} %loads_hbm.1, s32[4,256]{1,0:T(4,128)} %order_hbm.1, s32[4,8]{1,0:T(4,128)} %bitcast.1, bf16[8,4,2,64,256]{4,3,2,1,0:T(8,128)(2,1)} %factors_hbm.1), custom_call_target="tpu_custom_call" | custom-call | tf_op jit(solution)/shard_map/pallas_call | solution.py:392
  34.6 0.6 %copy.6 = f32[4,4,256]{2,1,0:T(4,128)} copy(f32[4,4,256]{2,1,0:T(4,128)S(1)} %shard_map.46) | data formatting | bytes 32768

commit v4 on v3

--- a/solution.py
+++ b/solution.py
@@ -69,16 +69,19 @@
         return leaf + step - 2 * step * ((leaf // step) % 2)
 
     def other_rank(away):
-        return (rank + away) % ranks
+        bit = ranks - away
+        to = rank
+        step = 1
+        while step < ranks:
+            if bit // step % 2:
+                to = to + step - 2 * step * ((rank // step) % 2)
+            step *= 2
+        return to
 
     barrier = pltpu.get_barrier_semaphore()
     remote_bits = sorted({bit for bit in level_bits if bit >= local_bits})
-    for away in range(1, ranks):
-        pl.semaphore_signal(
-            barrier, inc=1, device_id={"leaf": leaf, "rank": other_rank(away)}, device_id_type=MESH
-        )
     for bit in remote_bits:
-        for away in range(ranks):
+        for away in range(1, ranks + 1):
             pl.semaphore_signal(
                 barrier,
                 inc=1,
@@ -86,6 +89,10 @@
                 device_id_type=MESH,
             )
 
+    for away in range(1, ranks):
+        pl.semaphore_signal(
+            barrier, inc=1, device_id={"leaf": leaf, "rank": other_rank(away)}, device_id_type=MESH
+        )
     fetches = [
         pltpu.make_async_copy(order_hbm, order_ref, in_sem.at[0]),
         pltpu.make_async_copy(loads_hbm, loads_ref, in_sem.at[1]),
@@ -319,11 +326,11 @@
                 ).start()
 
             for away in range(1, ranks):
-                send_whole(rank, leaf, other_rank(away))
                 if with_partner:
                     send_whole(
                         ranks + rank, partner_leaf(level_bits[then]), other_rank(away)
                     )
+                send_whole(rank, leaf, other_rank(away))
             if with_partner:
                 send_whole(ranks + rank, partner_leaf(level_bits[then]), rank)
             for copy in bulk[then]:
@@ -337,11 +344,11 @@
                 send[then, 1, at] = partner[at]
         for away in range(1, ranks):
             to = other_rank(away)
-            remote(then, send.at[then, 0, to], rank, leaf, to).start()
             if with_partner:
                 remote(
                     then, send.at[then, 1, to], ranks + rank, partner_leaf(level_bits[then]), to
                 ).start()
+            remote(then, send.at[then, 0, to], rank, leaf, to).start()
         if with_partner:
             remote(
                 then, send.at[then, 1, rank], ranks + rank, partner_leaf(level_bits[then]), rank

time: 35.3 us -> 34.6 us (0.980)
  Pallas kernels: 34.6 us -> 33.9 us
    pallas_call x1, Pallas kernels: 34.6 us -> 33.9 us  [local(): pl.pallas_call(functools.partial(kernel, leaves, ranks), out_shape=pltpu....]
where the time goes in v4:
time: 34.6 us; the launch traced here: 34.5 us
  Pallas kernels  33.9 us (98%)
  local copies, waits for them, and re-layouts  0.61 us (2%)
    pallas_call x1, Pallas kernels, local(): pl.pallas_call(functools.partial(kernel, leaves, ranks), out_shape=pltpu....  33.9 us

profile of v4, /device:TPU:0, one launch (start us, length us, event | category | flops | bytes accessed | tf_op | source)
XLA Modules:
  0.0 34.5 jit_solution(2162854452579613940)
XLA Ops:
  0.0 33.9 %shard_map.46 = f32[4,4,256]{2,1,0:T(4,128)S(1)} custom-call(bf16[4,4,256]{2,1,0:T(4,128)(2,1)} %loads_hbm.1, s32[4,256]{1,0:T(4,128)} %order_hbm.1, s32[4,8]{1,0:T(4,128)} %bitcast.1, bf16[8,4,2,64,256]{4,3,2,1,0:T(8,128)(2,1)} %factors_hbm.1), custom_call_target="tpu_custom_call" | custom-call | tf_op jit(solution)/shard_map/pallas_call | solution.py:399
  33.9 0.6 %copy.6 = f32[4,4,256]{2,1,0:T(4,128)} copy(f32[4,4,256]{2,1,0:T(4,128)S(1)} %shard_map.46) | data formatting | bytes 32768
